TPU v7x, 128 devices: a whole 4x4x4 slice. The times are simulated.
128 devices in a mesh: gx: 16 (over z, x), gy: 8 (over y, core).
Axes of the slice: x: 4, y: 4, z: 4, core: 2. Of those that a mesh axis runs over, the one named last changes fastest.
Arguments:
- flow_field: float32 [1024, 4, 512], P(('gx', 'gy')), may hold values from -6 to 6
- enc_first: float32 [4, 128], replicated, may hold values from -3 to 3
- enc_second: bfloat16 [128, 128], replicated, may hold values from -0.5 to 0.5
- send_rows: int32 [128, 128, 8], P(('gx', 'gy')), may hold values from 0 to 512, as said below
- part_sizes: int32 [128, 128], P(('gx', 'gy')), may hold values from 0 to 8, as said below
- halo_rows: int32 [128, 2, 2, 64], P(('gx', 'gy')), may hold values from 0 to 1023, as said below
- neighbours: int32 [8, 131072], P(None, ('gx', 'gy')), may hold values from 0 to 1536, as said below
- edge_first: bfloat16 [2, 384, 128], replicated, may hold values from -0.3125 to 0.3125
- edge_second: bfloat16 [2, 128, 128], replicated, may hold values from -0.5 to 0.5
- node_first: bfloat16 [2, 256, 128], replicated, may hold values from -0.375 to 0.375
- node_second: bfloat16 [2, 128, 128], replicated, may hold values from -0.5 to 0.5
Outputs:
- node_latents: bfloat16 [131072, 128], P(('gx', 'gy'))
Inputs may be any that keep to these rules, and one draw needn't show every extreme that they name: For every source s and target d, send_rows[s, d, k] is a node of s for k < part_sizes[d, s] and 512 for the other slots; every node of s stands exactly once in send_rows[s]. part_sizes[d, s] is the number of nodes that device s sends to device d; the sum over d is 512 for every s; in every draw some device d receives 8 nodes from every source. `halo_rows`: every entry is an occupied slot of the device's graph nodes (s*8+k with k < part_sizes[d, s]); entries may repeat. `neighbours`: each entry is 1537 - 1 (no edge), an occupied slot of the device's own graph nodes, or a received halo row 1024 .. 1535; empty slots have no edges; every occupied node has 4 to 8 edges in its first slots, and some node of every device has 8.
All inputs are finite; a program needn't handle non-finite values.
Results may differ from a plain program's by a relative error of at most 0.015.
Values may be sent and summed in bfloat16 or wider, within the bound.
A program may use at most 64 MiB of HBM per device.

v0:
```python
import functools

import jax
import jax.numpy as jnp
import numpy as np
from jax import lax
from jax.experimental import pallas as pl
from jax.experimental.pallas import tpu as pltpu
from jax.sharding import PartitionSpec as P

MESH = pl.DeviceIdType.MESH
F32 = jnp.float32
BF16 = jnp.bfloat16
F8 = jnp.float8_e4m3fn

LAYERS = 2
GLL_POINTS = (
    -1.0,
    -0.8717401485096066,
    -0.5917001814331423,
    -0.2092992179024789,
    0.2092992179024789,
    0.5917001814331423,
    0.8717401485096066,
    1.0,
)
EPS = 1e-05
D = 128
NODES = 1024
HALO = 512
ROWS = NODES + HALO
SLOTS = 8
EDGES = SLOTS * NODES
CH = 512
STEPS = EDGES // CH
HALF = NODES // CH


def interp_table():
    gll_nodes = np.array(GLL_POINTS)
    targets = np.array([-0.75, -0.25, 0.25, 0.75])
    basis_line = np.ones((4, 8))
    for j in range(8):
        for m in range(8):
            if m != j:
                basis_line[:, j] *= (targets - gll_nodes[m]) / (gll_nodes[j] - gll_nodes[m])
    return np.kron(np.kron(basis_line, basis_line), basis_line).astype(np.float32)


def interp_parts():
    table = interp_table()
    high = table.astype(BF16)
    low = (table - high.astype(np.float32)).astype(BF16)
    return np.concatenate([high, low], axis=0)


def mm(a, b):
    return jnp.dot(a, b, preferred_element_type=F32)


def mm_t(a, b):
    return lax.dot_general(a, b, (((1,), (1,)), ((), ())), preferred_element_type=F32)


def two_terms(x, dtype):
    high = x.astype(dtype)
    return high, (x - high.astype(F32)).astype(dtype)


def half_silu(u):
    return u + u * jnp.tanh(u)


def norm_columns(v):
    spread = jnp.sum(v * v, axis=0, keepdims=True) * (1.0 / D)
    return v * lax.rsqrt(spread + EPS)


def centred_t(w):
    w = w.astype(F32)
    return (w - jnp.mean(w, axis=1, keepdims=True)).T.astype(BF16)


def scaled_t(w, scale):
    return (w.astype(F32).T * scale).astype(BF16)


def kernel(
    nx,
    ny,
    flow,
    interp,
    enc_first,
    enc_second,
    send_rows,
    halo,
    links,
    edge_first,
    edge_second,
    node_first,
    node_second,
    out,
    oht,
    e8,
    e16,
    part,
    t8,
    ohh,
    xs,
    wsrc,
    wown,
    wdst,
    we2,
    wn1,
    wn2,
    wenc1,
    wenc2,
    src,
    sbuf,
    r1,
    r2,
    hsend,
    hrecv,
    bsend,
    brecv,
    s1,
    q1,
    s2,
    q2,
    fs,
    fq,
    bs,
    bq,
):
    gx, gy = lax.axis_index("gx"), lax.axis_index("gy")

    def at_x(step):
        return (lax.rem(gx + (step + nx), nx), gy)

    def at_y(step):
        return (gx, lax.rem(gy + (step + ny), ny))

    barrier = pltpu.get_barrier_semaphore()
    for step in range(1, ny):
        pl.semaphore_signal(barrier, inc=1, device_id=at_y(step), device_id_type=MESH)
    for step in range(1, nx):
        pl.semaphore_signal(barrier, inc=1, device_id=at_x(step), device_id_type=MESH)

    tiles = []
    for e in range(8):
        f = flow[e]
        f = jnp.concatenate([f, f], axis=0)
        tiles.append(jnp.concatenate([f, f, f, f], axis=0))
    flow_high, flow_low = two_terms(jnp.concatenate(tiles, axis=0), BF16)
    main = mm_t(interp[...], flow_high)
    sampled = main[:64] + main[64:] + mm_t(interp[0:64, :], flow_low)
    columns = jnp.concatenate([sampled[:, 32 * e : 32 * e + 32] for e in range(8)], axis=0)
    col_high, col_low = two_terms(columns, BF16)
    table = jnp.concatenate(
        [
            col_high,
            jnp.ones((512, 8), BF16),
            jnp.zeros((512, 88), BF16),
            col_low,
            jnp.zeros((512, 96), BF16),
        ],
        axis=1,
    )
    lane = lax.broadcasted_iota(jnp.int32, (D, D), 1)
    picked = jnp.zeros((D, D), F32)
    slots = jnp.concatenate(
        [send_rows[0, pl.ds(y, nx, stride=ny), :] for y in range(ny)], axis=0
    )
    node_ids = lax.broadcasted_iota(jnp.int32, (D, 512), 1)
    for k in range(SLOTS):
        choose = (slots[:, k : k + 1] == node_ids).astype(F32).astype(BF16)
        both = mm(choose, table)
        mine = ((lane < 32) & (lane // 4 == k)) | (lane == 32 + k)
        picked = picked + jnp.where(mine, both[:, :D] + both[:, D:], 0.0)
    for y in range(ny):
        for x in range(nx):
            row = y * nx + x
            sbuf[y, x] = picked[row : row + 1, :]

    pl.semaphore_wait(barrier, nx + ny - 2)

    first = []
    for step in range(1, ny):
        target = at_y(step)
        copy = pltpu.make_async_remote_copy(
            src_ref=sbuf.at[target[1]],
            dst_ref=r1.at[:, gy],
            send_sem=s1.at[step - 1],
            recv_sem=q1.at[step - 1],
            device_id=target,
            device_id_type=MESH,
        )
        copy.start()
        first.append(copy)
    r1[:, gy] = sbuf[gy]

    sub8 = lax.broadcasted_iota(jnp.int32, (D, CH), 0).astype(jnp.int8)

    def make_oht(c, carry):
        k, half = c // HALF, lax.rem(c, HALF)
        ids = links[pl.ds(k, 1), pl.ds(pl.multiple_of(half * CH, CH), CH)]
        where = pl.ds(pl.multiple_of(c * CH, CH), CH)
        for a in range(ROWS // D):
            key = ids - D * a
            key = jnp.where((key >= 0) & (key < D), key, -1).astype(jnp.int8)
            oht[pl.ds(a * D, D), where] = jnp.where(
                key == sub8, jnp.ones((), F8), jnp.zeros((), F8)
            )
        return carry

    lax.fori_loop(0, STEPS // 2, make_oht, 0)

    for copy in first:
        copy.wait_recv()
    second = []
    for step in range(1, nx):
        target = at_x(step)
        copy = pltpu.make_async_remote_copy(
            src_ref=r1.at[target[0]],
            dst_ref=r2.at[gx],
            send_sem=s2.at[step - 1],
            recv_sem=q2.at[step - 1],
            device_id=target,
            device_id_type=MESH,
        )
        copy.start()
        second.append(copy)
    r2[gx] = r1[gx]

    lax.fori_loop(STEPS // 2, STEPS, make_oht, 0)

    spread_first = jnp.concatenate([enc_first[...], enc_first[...]], axis=0)
    spread_first = jnp.concatenate([spread_first] * 16, axis=0).T
    enc_high, enc_low = two_terms(jnp.where(lane < 32, spread_first * 0.5, 0.0), BF16)
    wenc1[0:D, 0:D] = enc_high
    wenc1[0:D, D : 2 * D] = enc_high
    wenc1[D : 2 * D, 0:D] = enc_low
    wenc1[D : 2 * D, D : 2 * D] = jnp.zeros((D, D), BF16)
    mark = lax.broadcasted_iota(jnp.int32, (16, 2 * D), 1)
    wenc1[2 * D : 2 * D + 16, :] = ((mark >= 32) & (mark < 40)).astype(F32).astype(BF16)
    wenc2[...] = centred_t(enc_second[...])
    for l in range(LAYERS):
        wown[l] = scaled_t(edge_first[l, 0:D, :], 4.0)
        wsrc[l] = scaled_t(edge_first[l, D : 2 * D, :], 4.0)
        wdst[l] = scaled_t(edge_first[l, 2 * D : 3 * D, :], 4.0)
        we2[l] = centred_t(edge_second[l])
        wn1[l, :, 0:D] = scaled_t(node_first[l, 0:D, :], 0.5)
        wn1[l, :, D : 2 * D] = scaled_t(node_first[l, D : 2 * D, :], 0.5)
        wn2[l] = centred_t(node_second[l])

    node_rows = lax.broadcasted_iota(jnp.int32, (NODES, D), 0)
    for j, (p, q) in enumerate((((1, 0), (1, 1)), ((0, 0), (0, 1)), ((0, 1), (1, 1)), ((0, 0), (1, 0)))):
        ids = jnp.concatenate([halo[0, p[0], p[1] : p[1] + 1, :], halo[0, q[0], q[1] : q[1] + 1, :]], axis=1)
        ohh[:, D * j : D * j + D] = (ids == node_rows).astype(F32).astype(BF16)

    for copy in first:
        copy.wait_send()
    for copy in second:
        copy.wait_recv()

    sub = lax.broadcasted_iota(jnp.int32, (8, D), 0)
    lane8 = lax.broadcasted_iota(jnp.int32, (8, D), 1)
    keep = ((lane8 < 32) & (lane8 // 4 == sub)) | (lane8 == 32 + sub)
    for x in range(nx):
        for y in range(0, ny, 2):
            rows = jnp.concatenate(
                [
                    jnp.where(keep, jnp.broadcast_to(r2[x, y], (8, D)), 0.0),
                    jnp.where(keep, jnp.broadcast_to(r2[x, y + 1], (8, D)), 0.0),
                ],
                axis=0,
            )
            high, low = two_terms(rows, BF16)
            base = (x * ny + y) * 8
            xs[base : base + 16, 0:D] = high
            xs[base : base + 16, D : 2 * D] = low
    pre = mm_t(wenc1[...], xs[...])
    filled = pre[2 * D : 2 * D + 1, :] > 0.5
    hidden = half_silu(pre[:D] + pre[D : 2 * D]).astype(BF16)
    h = norm_columns(mm(wenc2[...], hidden))
    h = jnp.where(filled, h, 0.0).astype(BF16)
    for copy in second:
        copy.wait_send()

    forward = (at_x(1), at_x(-1), at_y(1), at_y(-1))
    backward = (at_x(-1), at_x(1), at_y(-1), at_y(1))

    for l in range(LAYERS):
        proj = mm(wdst[l], h)
        border = mm(proj.astype(BF16), ohh[...]).astype(BF16)
        copies = []
        for j in range(4):
            hsend[l, j] = border[:, D * j : D * j + D]
            copy = pltpu.make_async_remote_copy(
                src_ref=hsend.at[l, j],
                dst_ref=hrecv.at[l, j],
                send_sem=fs.at[l, j],
                recv_sem=fq.at[l, j],
                device_id=forward[j],
                device_id_type=MESH,
            )
            copy.start()
            copies.append(copy)
        high, low = two_terms(proj, F8)
        t8[0:D, 0:NODES] = high
        t8[D : 2 * D, 0:NODES] = low
        src[...] = mm(wsrc[l], h)

        def local_step(c, carry):
            half = lax.rem(c, HALF)
            where = pl.ds(pl.multiple_of(c * CH, CH), CH)
            got = mm(t8[:, 0:NODES], oht[0:NODES, where])
            u = got[:D] + got[D:] + src[:, pl.ds(pl.multiple_of(half * CH, CH), CH)]
            if l > 0:
                u = u + mm(wown[l], e16[:, where])
            part[c] = u
            return carry

        lax.fori_loop(0, STEPS, local_step, 0)

        for j, copy in enumerate(copies):
            copy.wait_recv()
            high, low = two_terms(hrecv[l, j].astype(F32), F8)
            t8[0:D, NODES + D * j : NODES + D * j + D] = high
            t8[D : 2 * D, NODES + D * j : NODES + D * j + D] = low

        def edge_step(c, carry):
            where = pl.ds(pl.multiple_of(c * CH, CH), CH)
            got = mm(t8[:, NODES:ROWS], oht[NODES:ROWS, where])
            u = (part[c] + got[:D] + got[D:]) * 0.125
            new = norm_columns(mm(we2[l], half_silu(u).astype(BF16)))
            if l > 0:
                new = new + e16[:, where].astype(F32)
            if l + 1 < LAYERS:
                e16[:, where] = new.astype(BF16)
            high, low = two_terms(new * 16.0, F8)
            e8[0:D, where] = high
            e8[D : 2 * D, where] = low
            return carry

        lax.fori_loop(0, STEPS, edge_step, 0)

        sums = mm_t(e8[...], oht[NODES:ROWS, :])
        sums = ((sums[:D] + sums[D:]) * 0.0625).astype(BF16)
        back = []
        for j in range(4):
            bsend[l, j] = sums[:, D * j : D * j + D]
            copy = pltpu.make_async_remote_copy(
                src_ref=bsend.at[l, j],
                dst_ref=brecv.at[l, j],
                send_sem=bs.at[l, j],
                recv_sem=bq.at[l, j],
                device_id=backward[j],
                device_id_type=MESH,
            )
            copy.start()
            back.append(copy)
        sums = mm_t(e8[...], oht[0:NODES, :])
        sums = (sums[:D] + sums[D:]) * 0.0625
        for copy in back:
            copy.wait_recv()
        returned = jnp.concatenate([brecv[l, j] for j in range(4)], axis=1)
        sums = sums + mm_t(returned, ohh[...])
        pre = mm(wn1[l], jnp.concatenate([h, sums.astype(BF16)], axis=0))
        new = h.astype(F32) + norm_columns(mm(wn2[l], half_silu(pre).astype(BF16)))
        new = jnp.where(filled, new, 0.0)
        for copy in copies:
            copy.wait_send()
        for copy in back:
            copy.wait_send()
        if l + 1 < LAYERS:
            h = new.astype(BF16)
        else:
            out[...] = new.T.astype(BF16)


def solution(mesh):
    nx, ny = mesh.shape["gx"], mesh.shape["gy"]

    def shards(
        flow_field,
        enc_first,
        enc_second,
        send_rows,
        part_sizes,
        halo_rows,
        neighbours,
        edge_first,
        edge_second,
        node_first,
        node_second,
    ):
        del part_sizes
        vmem = pl.BlockSpec(memory_space=pltpu.VMEM)
        dma = pltpu.SemaphoreType.DMA
        return pl.pallas_call(
            functools.partial(kernel, nx, ny),
            out_shape=jax.ShapeDtypeStruct((NODES, D), BF16),
            in_specs=[vmem] * 11,
            out_specs=vmem,
            scratch_shapes=[
                pltpu.VMEM((ROWS, EDGES), F8),
                pltpu.VMEM((2 * D, EDGES), F8),
                pltpu.VMEM((D, EDGES), BF16),
                pltpu.VMEM((STEPS, D, CH), F32),
                pltpu.VMEM((2 * D, ROWS), F8),
                pltpu.VMEM((NODES, HALO), BF16),
                pltpu.VMEM((NODES, 2 * D), BF16),
                pltpu.VMEM((LAYERS, D, D), BF16),
                pltpu.VMEM((LAYERS, D, D), BF16),
                pltpu.VMEM((LAYERS, D, D), BF16),
                pltpu.VMEM((LAYERS, D, D), BF16),
                pltpu.VMEM((LAYERS, D, 2 * D), BF16),
                pltpu.VMEM((LAYERS, D, D), BF16),
                pltpu.VMEM((2 * D + 16, 2 * D), BF16),
                pltpu.VMEM((D, D), BF16),
                pltpu.VMEM((D, NODES), F32),
                pltpu.VMEM((ny, nx, 1, D), F32),
                pltpu.VMEM((nx, ny, 1, D), F32),
                pltpu.VMEM((nx, ny, 1, D), F32),
                pltpu.VMEM((LAYERS, 4, D, D), BF16),
                pltpu.VMEM((LAYERS, 4, D, D), BF16),
                pltpu.VMEM((LAYERS, 4, D, D), BF16),
                pltpu.VMEM((LAYERS, 4, D, D), BF16),
                dma((ny - 1,)),
                dma((ny - 1,)),
                dma((nx - 1,)),
                dma((nx - 1,)),
                dma((LAYERS, 4)),
                dma((LAYERS, 4)),
                dma((LAYERS, 4)),
                dma((LAYERS, 4)),
            ],
            compiler_params=pltpu.CompilerParams(
                collective_id=0, has_side_effects=True, vmem_limit_bytes=48 << 20
            ),
        )(
            flow_field,
            jnp.asarray(interp_parts()),
            enc_first,
            enc_second,
            send_rows,
            halo_rows,
            neighbours,
            edge_first,
            edge_second,
            node_first,
            node_second,
        )

    in_specs = (
        P(("gx", "gy"), None, None),
        P(),
        P(),
        P(("gx", "gy"), None, None),
        P(("gx", "gy"), None),
        P(("gx", "gy"), None, None, None),
        P(None, ("gx", "gy")),
        P(),
        P(),
        P(),
        P(),
    )
    out_specs = P(("gx", "gy"), None)
    return jax.shard_map(shards, mesh=mesh, in_specs=in_specs, out_specs=out_specs, check_vma=False)
```

profile of v0, /device:TPU:0, one launch (start us, length us, event | category | flops | bytes accessed | tf_op | source)
XLA Modules:
  0.0 64.7 jit_solution(4910837515300176936)
XLA Ops:
  0.0 0.0 copy-start.9
  0.0 0.0 copy-start.8
  0.0 0.0 copy-start.3
  0.0 0.8 %copy.12.send_rows = s32[1,128,8]{2,1,0:T(8,128)S(1)} copy(s32[1,128,8]{1,2,0:T(8,128)} %param.15) | data formatting | bytes 8192 | tf_op args[3]
  0.8 0.0 copy-done.9
  0.8 0.0 copy-done.8
  0.8 0.0 copy-done.3
  0.9 0.0 copy-start
  0.9 0.9 %copy-done = bf16[2,384,128]{2,1,0:T(8,128)(2,1)S(1)} copy-done((bf16[2,384,128]{2,1,0:T(8,128)(2,1)S(1)}, bf16[2,384,128]{2,1,0:T(8,128)(2,1)}, u32[]{:S(2)}) %copy-start) | copy-done | bytes 196632
  1.8 0.0 copy-start.1
  1.8 0.9 %copy-done.1 = bf16[2,256,128]{2,1,0:T(8,128)(2,1)S(1)} copy-done((bf16[2,256,128]{2,1,0:T(8,128)(2,1)S(1)}, bf16[2,256,128]{2,1,0:T(8,128)(2,1)}, u32[]{:S(2)}) %copy-start.1) | copy-done | bytes 131096
  2.7 0.0 copy-start.2
  2.7 0.9 %copy-done.2 = bf16[128,512]{1,0:T(8,128)(2,1)S(1)} copy-done((bf16[128,512]{1,0:T(8,128)(2,1)S(1)}, bf16[128,512]{1,0:T(8,128)(2,1)}, u32[]{:S(2)}) %copy-start.2) | copy-done | bytes 131096
  3.6 0.0 copy-start.4
  3.6 0.8 %copy-done.4 = bf16[2,128,128]{2,1,0:T(8,128)(2,1)S(1)} copy-done((bf16[2,128,128]{2,1,0:T(8,128)(2,1)S(1)}, bf16[2,128,128]{2,1,0:T(8,128)(2,1)}, u32[]{:S(2)}) %copy-start.4) | copy-done | bytes 65560
  4.5 0.0 copy-start.5
  4.5 0.8 %copy-done.5 = bf16[2,128,128]{2,1,0:T(8,128)(2,1)S(1)} copy-done((bf16[2,128,128]{2,1,0:T(8,128)(2,1)S(1)}, bf16[2,128,128]{2,1,0:T(8,128)(2,1)}, u32[]{:S(2)}) %copy-start.5) | copy-done | bytes 65560
  5.3 0.0 copy-start.6
  5.3 0.8 %copy-done.6 = bf16[128,128]{1,0:T(8,128)(2,1)S(1)} copy-done((bf16[128,128]{1,0:T(8,128)(2,1)S(1)}, bf16[128,128]{1,0:T(8,128)(2,1)}, u32[]{:S(2)}) %copy-start.6) | copy-done | bytes 32792
  6.1 0.0 copy-start.7
  6.1 0.8 %copy-done.7 = s32[8,1024]{1,0:T(8,128)S(1)} copy-done((s32[8,1024]{1,0:T(8,128)S(1)}, s32[8,1024]{1,0:T(8,128)}, u32[]{:S(2)}) %copy-start.7) | copy-done | bytes 32792
  6.8 57.2 %shard_map.109 = bf16[1024,128]{1,0:T(8,128)(2,1)S(1)} custom-call(f32[8,4,512]{2,1,0:T(4,128)S(1)} %copy-done.3, bf16[128,512]{1,0:T(8,128)(2,1)S(1)} %copy-done.2, f32[4,128]{1,0:T(4,128)S(1)} %copy-done.8, bf16[128,128]{1,0:T(8,128)(2,1)S(1)} %copy-done.6, s32[1,128,8]{2,1,0:T(8,128)S(1)} %copy.12.send_rows, s32[1,2,2,64]{3,2,1,0:T(2,128)S(1)} %copy-done.9, ...), custom_call_target="tpu_custom_call" | custom-call | tf_op jit(solution)/shard_map/pallas_call | solution.py:401
  64.0 0.7 %copy.14 = bf16[1024,128]{1,0:T(8,128)(2,1)} copy(bf16[1024,128]{1,0:T(8,128)(2,1)S(1)} %shard_map.109) | data formatting | bytes 524288
Async XLA Ops:
  0.0 0.8 %copy-start.9 = (s32[1,2,2,64]{3,2,1,0:T(2,128)S(1)}, s32[1,2,2,64]{3,2,1,0:T(2,128)}, u32[]{:S(2)}) copy-start(s32[1,2,2,64]{3,2,1,0:T(2,128)} %halo.1) | copy-start | bytes 3076
  0.0 0.8 %copy-start.8 = (f32[4,128]{1,0:T(4,128)S(1)}, f32[4,128]{1,0:T(4,128)}, u32[]{:S(2)}) copy-start(f32[4,128]{1,0:T(4,128)} %enc_first.1) | copy-start | bytes 6148
  0.0 0.9 %copy-start.3 = (f32[8,4,512]{2,1,0:T(4,128)S(1)}, f32[8,4,512]{2,1,0:T(4,128)}, u32[]{:S(2)}) copy-start(f32[8,4,512]{2,1,0:T(4,128)} %flow.1) | copy-start | bytes 196612
  0.9 0.9 %copy-start = (bf16[2,384,128]{2,1,0:T(8,128)(2,1)S(1)}, bf16[2,384,128]{2,1,0:T(8,128)(2,1)}, u32[]{:S(2)}) copy-start(bf16[2,384,128]{2,1,0:T(8,128)(2,1)} %edge_first.1) | copy-start | bytes 589828
  1.8 0.9 %copy-start.1 = (bf16[2,256,128]{2,1,0:T(8,128)(2,1)S(1)}, bf16[2,256,128]{2,1,0:T(8,128)(2,1)}, u32[]{:S(2)}) copy-start(bf16[2,256,128]{2,1,0:T(8,128)(2,1)} %node_first.1) | copy-start | bytes 393220
  2.7 0.9 %copy-start.2 = (bf16[128,512]{1,0:T(8,128)(2,1)S(1)}, bf16[128,512]{1,0:T(8,128)(2,1)}, u32[]{:S(2)}) copy-start(bf16[128,512]{1,0:T(8,128)(2,1)} %constant.2.clone.interp) | copy-start | bytes 393220
  3.6 0.8 %copy-start.4 = (bf16[2,128,128]{2,1,0:T(8,128)(2,1)S(1)}, bf16[2,128,128]{2,1,0:T(8,128)(2,1)}, u32[]{:S(2)}) copy-start(bf16[2,128,128]{2,1,0:T(8,128)(2,1)} %edge_second.1) | copy-start | bytes 196612
  4.5 0.8 %copy-start.5 = (bf16[2,128,128]{2,1,0:T(8,128)(2,1)S(1)}, bf16[2,128,128]{2,1,0:T(8,128)(2,1)}, u32[]{:S(2)}) copy-start(bf16[2,128,128]{2,1,0:T(8,128)(2,1)} %node_second.1) | copy-start | bytes 196612
  5.3 0.8 %copy-start.6 = (bf16[128,128]{1,0:T(8,128)(2,1)S(1)}, bf16[128,128]{1,0:T(8,128)(2,1)}, u32[]{:S(2)}) copy-start(bf16[128,128]{1,0:T(8,128)(2,1)} %enc_second.1) | copy-start | bytes 98308
  6.1 0.8 %copy-start.7 = (s32[8,1024]{1,0:T(8,128)S(1)}, s32[8,1024]{1,0:T(8,128)}, u32[]{:S(2)}) copy-start(s32[8,1024]{1,0:T(8,128)} %links.1) | copy-start | bytes 98308
where the time goes:
time: 65.2 us; the launch traced here: 64.7 us
  Pallas kernels  57.2 us (88%)
  local copies, waits for them, and re-layouts  7.51 us (12%)
    pallas_call x1, Pallas kernels, shards(): pl.pallas_call(functools.partial(kernel, nx, ny), out_shape=jax.ShapeDtyp...  57.2 us
    unnamed x22, local copies, waits for them, and re-layouts  7.51 us

commit v1 on v0

--- a/solution.py
+++ b/solution.py
@@ -31,9 +31,9 @@
 ROWS = NODES + HALO
 SLOTS = 8
 EDGES = SLOTS * NODES
-CH = 512
-STEPS = EDGES // CH
-HALF = NODES // CH
+GROUP = 4
+CH = GROUP * NODES
+STEPS = SLOTS // GROUP
 
 
 def interp_table():
@@ -71,9 +71,9 @@
     return u + u * jnp.tanh(u)
 
 
-def norm_columns(v):
+def norm_columns(v, scale=1.0):
     spread = jnp.sum(v * v, axis=0, keepdims=True) * (1.0 / D)
-    return v * lax.rsqrt(spread + EPS)
+    return v * (lax.rsqrt(spread + EPS) * scale)
 
 
 def centred_t(w):
@@ -88,18 +88,29 @@
 def kernel(
     nx,
     ny,
+    flow_hbm,
+    interp_hbm,
+    send_hbm,
+    links_hbm,
+    halo_hbm,
+    enc_first_hbm,
+    enc_second_hbm,
+    edge_first_hbm,
+    edge_second_hbm,
+    node_first_hbm,
+    node_second_hbm,
+    out,
     flow,
     interp,
+    send_rows,
+    links,
+    halo,
     enc_first,
     enc_second,
-    send_rows,
-    halo,
-    links,
     edge_first,
     edge_second,
     node_first,
     node_second,
-    out,
     oht,
     e8,
     e16,
@@ -116,13 +127,16 @@
     wenc1,
     wenc2,
     src,
+    ordered,
     sbuf,
     r1,
+    mid,
     r2,
     hsend,
     hrecv,
     bsend,
     brecv,
+    loads,
     s1,
     q1,
     s2,
@@ -145,6 +159,27 @@
         pl.semaphore_signal(barrier, inc=1, device_id=at_y(step), device_id_type=MESH)
     for step in range(1, nx):
         pl.semaphore_signal(barrier, inc=1, device_id=at_x(step), device_id_type=MESH)
+
+    pairs = (
+        (flow_hbm, flow),
+        (interp_hbm, interp),
+        (send_hbm, send_rows),
+        (links_hbm, links),
+        (halo_hbm, halo),
+        (enc_first_hbm, enc_first),
+        (enc_second_hbm, enc_second),
+        (edge_first_hbm, edge_first),
+        (edge_second_hbm, edge_second),
+        (node_first_hbm, node_first),
+        (node_second_hbm, node_second),
+    )
+    loading = [
+        pltpu.make_async_copy(there, here, loads.at[i]) for i, (there, here) in enumerate(pairs)
+    ]
+    for copy in loading:
+        copy.start()
+    for copy in loading[:3]:
+        copy.wait()
 
     tiles = []
     for e in range(8):
@@ -168,8 +203,9 @@
     )
     lane = lax.broadcasted_iota(jnp.int32, (D, D), 1)
     picked = jnp.zeros((D, D), F32)
+    ordered[...] = jnp.concatenate([send_rows[0]] * 16, axis=0).T
     slots = jnp.concatenate(
-        [send_rows[0, pl.ds(y, nx, stride=ny), :] for y in range(ny)], axis=0
+        [ordered[pl.ds(y, nx, stride=ny), :] for y in range(ny)], axis=0
     )
     node_ids = lax.broadcasted_iota(jnp.int32, (D, 512), 1)
     for k in range(SLOTS):
@@ -178,9 +214,7 @@
         mine = ((lane < 32) & (lane // 4 == k)) | (lane == 32 + k)
         picked = picked + jnp.where(mine, both[:, :D] + both[:, D:], 0.0)
     for y in range(ny):
-        for x in range(nx):
-            row = y * nx + x
-            sbuf[y, x] = picked[row : row + 1, :]
+        sbuf[y] = picked[y * nx : y * nx + nx, :]
 
     pl.semaphore_wait(barrier, nx + ny - 2)
 
@@ -189,7 +223,7 @@
         target = at_y(step)
         copy = pltpu.make_async_remote_copy(
             src_ref=sbuf.at[target[1]],
-            dst_ref=r1.at[:, gy],
+            dst_ref=r1.at[gy],
             send_sem=s1.at[step - 1],
             recv_sem=q1.at[step - 1],
             device_id=target,
@@ -197,31 +231,34 @@
         )
         copy.start()
         first.append(copy)
-    r1[:, gy] = sbuf[gy]
-
-    sub8 = lax.broadcasted_iota(jnp.int32, (D, CH), 0).astype(jnp.int8)
-
-    def make_oht(c, carry):
-        k, half = c // HALF, lax.rem(c, HALF)
-        ids = links[pl.ds(k, 1), pl.ds(pl.multiple_of(half * CH, CH), CH)]
-        where = pl.ds(pl.multiple_of(c * CH, CH), CH)
+    r1[gy] = sbuf[gy]
+    for copy in loading[3:]:
+        copy.wait()
+
+    sub8 = lax.broadcasted_iota(jnp.int32, (D, NODES), 0).astype(jnp.int8)
+
+    def make_oht(k, carry):
+        ids = links[pl.ds(k, 1), :]
+        where = pl.ds(pl.multiple_of(k * NODES, NODES), NODES)
         for a in range(ROWS // D):
             key = ids - D * a
             key = jnp.where((key >= 0) & (key < D), key, -1).astype(jnp.int8)
             oht[pl.ds(a * D, D), where] = jnp.where(
-                key == sub8, jnp.ones((), F8), jnp.zeros((), F8)
+                key == sub8, jnp.full((), 0.125, F8), jnp.zeros((), F8)
             )
         return carry
 
-    lax.fori_loop(0, STEPS // 2, make_oht, 0)
+    lax.fori_loop(0, SLOTS // 2, make_oht, 0)
 
     for copy in first:
         copy.wait_recv()
+    for x in range(nx):
+        mid[x] = r1[:, x, :]
     second = []
     for step in range(1, nx):
         target = at_x(step)
         copy = pltpu.make_async_remote_copy(
-            src_ref=r1.at[target[0]],
+            src_ref=mid.at[target[0]],
             dst_ref=r2.at[gx],
             send_sem=s2.at[step - 1],
             recv_sem=q2.at[step - 1],
@@ -230,9 +267,9 @@
         )
         copy.start()
         second.append(copy)
-    r2[gx] = r1[gx]
-
-    lax.fori_loop(STEPS // 2, STEPS, make_oht, 0)
+    r2[gx] = mid[gx]
+
+    lax.fori_loop(SLOTS // 2, SLOTS, make_oht, 0)
 
     spread_first = jnp.concatenate([enc_first[...], enc_first[...]], axis=0)
     spread_first = jnp.concatenate([spread_first] * 16, axis=0).T
@@ -245,8 +282,8 @@
     wenc1[2 * D : 2 * D + 16, :] = ((mark >= 32) & (mark < 40)).astype(F32).astype(BF16)
     wenc2[...] = centred_t(enc_second[...])
     for l in range(LAYERS):
-        wown[l] = scaled_t(edge_first[l, 0:D, :], 4.0)
-        wsrc[l] = scaled_t(edge_first[l, D : 2 * D, :], 4.0)
+        wown[l] = scaled_t(edge_first[l, 0:D, :], 0.03125)
+        wsrc[l] = scaled_t(edge_first[l, D : 2 * D, :], 0.5)
         wdst[l] = scaled_t(edge_first[l, 2 * D : 3 * D, :], 4.0)
         we2[l] = centred_t(edge_second[l])
         wn1[l, :, 0:D] = scaled_t(node_first[l, 0:D, :], 0.5)
@@ -270,8 +307,8 @@
         for y in range(0, ny, 2):
             rows = jnp.concatenate(
                 [
-                    jnp.where(keep, jnp.broadcast_to(r2[x, y], (8, D)), 0.0),
-                    jnp.where(keep, jnp.broadcast_to(r2[x, y + 1], (8, D)), 0.0),
+                    jnp.where(keep, jnp.broadcast_to(r2[x, y : y + 1, :], (8, D)), 0.0),
+                    jnp.where(keep, jnp.broadcast_to(r2[x, y + 1 : y + 2, :], (8, D)), 0.0),
                 ],
                 axis=0,
             )
@@ -312,16 +349,15 @@
         src[...] = mm(wsrc[l], h)
 
         def local_step(c, carry):
-            half = lax.rem(c, HALF)
             where = pl.ds(pl.multiple_of(c * CH, CH), CH)
             got = mm(t8[:, 0:NODES], oht[0:NODES, where])
-            u = got[:D] + got[D:] + src[:, pl.ds(pl.multiple_of(half * CH, CH), CH)]
+            u = got[:D] + got[D:] + jnp.concatenate([src[...]] * GROUP, axis=1)
             if l > 0:
                 u = u + mm(wown[l], e16[:, where])
             part[c] = u
             return carry
 
-        lax.fori_loop(0, STEPS, local_step, 0)
+        lax.fori_loop(0, STEPS, local_step, 0, unroll=2)
 
         for j, copy in enumerate(copies):
             copy.wait_recv()
@@ -332,21 +368,21 @@
         def edge_step(c, carry):
             where = pl.ds(pl.multiple_of(c * CH, CH), CH)
             got = mm(t8[:, NODES:ROWS], oht[NODES:ROWS, where])
-            u = (part[c] + got[:D] + got[D:]) * 0.125
-            new = norm_columns(mm(we2[l], half_silu(u).astype(BF16)))
+            u = (part[c] + got[:D] + got[D:]).astype(BF16)
+            new = norm_columns(mm(we2[l], half_silu(u)), 16.0).astype(BF16)
             if l > 0:
-                new = new + e16[:, where].astype(F32)
+                new = new + e16[:, where]
             if l + 1 < LAYERS:
-                e16[:, where] = new.astype(BF16)
-            high, low = two_terms(new * 16.0, F8)
+                e16[:, where] = new
+            high = new.astype(F8)
             e8[0:D, where] = high
-            e8[D : 2 * D, where] = low
+            e8[D : 2 * D, where] = (new - high.astype(BF16)).astype(F8)
             return carry
 
-        lax.fori_loop(0, STEPS, edge_step, 0)
+        lax.fori_loop(0, STEPS, edge_step, 0, unroll=2)
 
         sums = mm_t(e8[...], oht[NODES:ROWS, :])
-        sums = ((sums[:D] + sums[D:]) * 0.0625).astype(BF16)
+        sums = ((sums[:D] + sums[D:]) * 0.5).astype(BF16)
         back = []
         for j in range(4):
             bsend[l, j] = sums[:, D * j : D * j + D]
@@ -361,7 +397,7 @@
             copy.start()
             back.append(copy)
         sums = mm_t(e8[...], oht[0:NODES, :])
-        sums = (sums[:D] + sums[D:]) * 0.0625
+        sums = (sums[:D] + sums[D:]) * 0.5
         for copy in back:
             copy.wait_recv()
         returned = jnp.concatenate([brecv[l, j] for j in range(4)], axis=1)
@@ -398,12 +434,26 @@
         del part_sizes
         vmem = pl.BlockSpec(memory_space=pltpu.VMEM)
         dma = pltpu.SemaphoreType.DMA
+        operands = (
+            flow_field,
+            jnp.asarray(interp_parts()),
+            jnp.transpose(send_rows, (0, 2, 1)),
+            neighbours,
+            halo_rows,
+            enc_first,
+            enc_second,
+            edge_first,
+            edge_second,
+            node_first,
+            node_second,
+        )
         return pl.pallas_call(
             functools.partial(kernel, nx, ny),
             out_shape=jax.ShapeDtypeStruct((NODES, D), BF16),
-            in_specs=[vmem] * 11,
+            in_specs=[pl.BlockSpec(memory_space=pltpu.HBM)] * 11,
             out_specs=vmem,
             scratch_shapes=[
+                *[pltpu.VMEM(x.shape, x.dtype) for x in operands],
                 pltpu.VMEM((ROWS, EDGES), F8),
                 pltpu.VMEM((2 * D, EDGES), F8),
                 pltpu.VMEM((D, EDGES), BF16),
@@ -420,13 +470,16 @@
                 pltpu.VMEM((2 * D + 16, 2 * D), BF16),
                 pltpu.VMEM((D, D), BF16),
                 pltpu.VMEM((D, NODES), F32),
-                pltpu.VMEM((ny, nx, 1, D), F32),
-                pltpu.VMEM((nx, ny, 1, D), F32),
-                pltpu.VMEM((nx, ny, 1, D), F32),
+                pltpu.VMEM((D, D), jnp.int32),
+                pltpu.VMEM((ny, nx, D), F32),
+                pltpu.VMEM((ny, nx, D), F32),
+                pltpu.VMEM((nx, ny, D), F32),
+                pltpu.VMEM((nx, ny, D), F32),
                 pltpu.VMEM((LAYERS, 4, D, D), BF16),
                 pltpu.VMEM((LAYERS, 4, D, D), BF16),
                 pltpu.VMEM((LAYERS, 4, D, D), BF16),
                 pltpu.VMEM((LAYERS, 4, D, D), BF16),
+                dma((len(operands),)),
                 dma((ny - 1,)),
                 dma((ny - 1,)),
                 dma((nx - 1,)),
@@ -437,21 +490,9 @@
                 dma((LAYERS, 4)),
             ],
             compiler_params=pltpu.CompilerParams(
-                collective_id=0, has_side_effects=True, vmem_limit_bytes=48 << 20
+                collective_id=0, has_side_effects=True, vmem_limit_bytes=60 << 20
             ),
-        )(
-            flow_field,
-            jnp.asarray(interp_parts()),
-            enc_first,
-            enc_second,
-            send_rows,
-            halo_rows,
-            neighbours,
-            edge_first,
-            edge_second,
-            node_first,
-            node_second,
-        )
+        )(*operands)
 
     in_specs = (
         P(("gx", "gy"), None, None),

time: 65.2 us -> 47 us (0.72)
  Pallas kernels: 57.2 us -> 45.2 us
  local copies, waits for them, and re-layouts: 7.51 us -> 1.67 us
    pallas_call x1, Pallas kernels: 57.2 us -> 45.2 us  [shards(): pl.pallas_call(functools.partial(kernel, nx, ny), out_shape=jax.ShapeDtyp...]
    unnamed x22 -> x1, local copies, waits for them, and re-layouts: 7.51 us -> 1.67 us
where the time goes in v1:
time: 47 us; the launch traced here: 46.9 us
  Pallas kernels  45.2 us (96%)
  local copies, waits for them, and re-layouts  1.67 us (4%)
    pallas_call x1, Pallas kernels, shards(): pl.pallas_call(functools.partial(kernel, nx, ny), out_shape=jax.ShapeDtyp...  45.2 us
    unnamed x1, local copies, waits for them, and re-layouts  1.67 us

profile of v1, /device:TPU:0, one launch (start us, length us, event | category | flops | bytes accessed | tf_op | source)
XLA Modules:
  0.0 46.9 jit_solution(4468186126081707102)
XLA Ops:
  0.0 45.2 %shard_map.109 = bf16[1024,128]{1,0:T(8,128)(2,1)} custom-call(f32[8,4,512]{2,1,0:T(4,128)} %flow_hbm.1, bf16[128,512]{1,0:T(8,128)(2,1)} %constant.2.clone.interp_hbm, s32[1,8,128]{2,1,0:T(8,128)} %bitcast.1, s32[8,1024]{1,0:T(8,128)} %links_hbm.1, s32[1,2,2,64]{3,2,1,0:T(2,128)} %halo_hbm.1, f32[4,128]{1,0:T(4,128)} %enc_first_hbm.1, ...), custom_call_target="tpu_custom_call" | custom-call | tf_op jit(solution)/shard_map/pallas_call | solution.py:450
  45.2 1.7 %copy.13 = bf16[1024,128]{1,0:T(8,128)(2,1)} copy(bf16[1024,128]{1,0:T(8,128)(2,1)} %shard_map.109) | data formatting | bytes 524288

commit v2 on v1

--- a/solution.py
+++ b/solution.py
@@ -29,6 +29,7 @@
 NODES = 1024
 HALO = 512
 ROWS = NODES + HALO
+FAR = NODES + HALO // 2
 SLOTS = 8
 EDGES = SLOTS * NODES
 GROUP = 4
@@ -154,12 +155,6 @@
     def at_y(step):
         return (gx, lax.rem(gy + (step + ny), ny))
 
-    barrier = pltpu.get_barrier_semaphore()
-    for step in range(1, ny):
-        pl.semaphore_signal(barrier, inc=1, device_id=at_y(step), device_id_type=MESH)
-    for step in range(1, nx):
-        pl.semaphore_signal(barrier, inc=1, device_id=at_x(step), device_id_type=MESH)
-
     pairs = (
         (flow_hbm, flow),
         (interp_hbm, interp),
@@ -178,6 +173,11 @@
     ]
     for copy in loading:
         copy.start()
+    barrier = pltpu.get_barrier_semaphore()
+    for step in range(1, ny):
+        pl.semaphore_signal(barrier, inc=1, device_id=at_y(step), device_id_type=MESH)
+    for step in range(1, nx):
+        pl.semaphore_signal(barrier, inc=1, device_id=at_x(step), device_id_type=MESH)
     for copy in loading[:3]:
         copy.wait()
 
@@ -329,10 +329,12 @@
 
     for l in range(LAYERS):
         proj = mm(wdst[l], h)
-        border = mm(proj.astype(BF16), ohh[...]).astype(BF16)
+        rounded = proj.astype(BF16)
         copies = []
         for j in range(4):
-            hsend[l, j] = border[:, D * j : D * j + D]
+            if j % 2 == 0:
+                border = mm(rounded, ohh[:, D * j : D * j + 2 * D]).astype(BF16)
+            hsend[l, j] = border[:, D * (j % 2) : D * (j % 2) + D]
             copy = pltpu.make_async_remote_copy(
                 src_ref=hsend.at[l, j],
                 dst_ref=hrecv.at[l, j],
@@ -359,15 +361,28 @@
 
         lax.fori_loop(0, STEPS, local_step, 0, unroll=2)
 
-        for j, copy in enumerate(copies):
-            copy.wait_recv()
+        def take(j):
+            copies[j].wait_recv()
             high, low = two_terms(hrecv[l, j].astype(F32), F8)
             t8[0:D, NODES + D * j : NODES + D * j + D] = high
             t8[D : 2 * D, NODES + D * j : NODES + D * j + D] = low
 
+        take(2)
+        take(3)
+
+        def near_step(c, carry):
+            where = pl.ds(pl.multiple_of(c * CH, CH), CH)
+            got = mm(t8[:, FAR:ROWS], oht[FAR:ROWS, where])
+            part[c] = part[c] + got[:D] + got[D:]
+            return carry
+
+        lax.fori_loop(0, STEPS, near_step, 0, unroll=2)
+        take(0)
+        take(1)
+
         def edge_step(c, carry):
             where = pl.ds(pl.multiple_of(c * CH, CH), CH)
-            got = mm(t8[:, NODES:ROWS], oht[NODES:ROWS, where])
+            got = mm(t8[:, NODES:FAR], oht[NODES:FAR, where])
             u = (part[c] + got[:D] + got[D:]).astype(BF16)
             new = norm_columns(mm(we2[l], half_silu(u)), 16.0).astype(BF16)
             if l > 0:
@@ -398,10 +413,11 @@
             back.append(copy)
         sums = mm_t(e8[...], oht[0:NODES, :])
         sums = (sums[:D] + sums[D:]) * 0.5
-        for copy in back:
-            copy.wait_recv()
-        returned = jnp.concatenate([brecv[l, j] for j in range(4)], axis=1)
-        sums = sums + mm_t(returned, ohh[...])
+        for j in (2, 0):
+            back[j].wait_recv()
+            back[j + 1].wait_recv()
+            returned = jnp.concatenate([brecv[l, j], brecv[l, j + 1]], axis=1)
+            sums = sums + mm_t(returned, ohh[:, D * j : D * j + 2 * D])
         pre = mm(wn1[l], jnp.concatenate([h, sums.astype(BF16)], axis=0))
         new = h.astype(F32) + norm_columns(mm(wn2[l], half_silu(pre).astype(BF16)))
         new = jnp.where(filled, new, 0.0)

time: 47 us -> 46.2 us (0.983)
  Pallas kernels: 45.2 us -> 44.3 us
    pallas_call x1, Pallas kernels: 45.2 us -> 44.3 us  [shards(): pl.pallas_call(functools.partial(kernel, nx, ny), out_shape=jax.ShapeDtyp...]
where the time goes in v2:
time: 46.2 us; the launch traced here: 46 us
  Pallas kernels  44.3 us (96%)
  local copies, waits for them, and re-layouts  1.67 us (4%)
    pallas_call x1, Pallas kernels, shards(): pl.pallas_call(functools.partial(kernel, nx, ny), out_shape=jax.ShapeDtyp...  44.3 us
    unnamed x1, local copies, waits for them, and re-layouts  1.67 us

profile of v2, /device:TPU:0, one launch (start us, length us, event | category | flops | bytes accessed | tf_op | source)
XLA Modules:
  0.0 46.0 jit_solution(5247437078714325218)
XLA Ops:
  0.0 44.3 %shard_map.109 = bf16[1024,128]{1,0:T(8,128)(2,1)} custom-call(f32[8,4,512]{2,1,0:T(4,128)} %flow_hbm.1, bf16[128,512]{1,0:T(8,128)(2,1)} %constant.2.clone.interp_hbm, s32[1,8,128]{2,1,0:T(8,128)} %bitcast.1, s32[8,1024]{1,0:T(8,128)} %links_hbm.1, s32[1,2,2,64]{3,2,1,0:T(2,128)} %halo_hbm.1, f32[4,128]{1,0:T(4,128)} %enc_first_hbm.1, ...), custom_call_target="tpu_custom_call" | custom-call | tf_op jit(solution)/shard_map/pallas_call | solution.py:466
  44.3 1.7 %copy.13 = bf16[1024,128]{1,0:T(8,128)(2,1)} copy(bf16[1024,128]{1,0:T(8,128)(2,1)} %shard_map.109) | data formatting | bytes 524288

commit v3 on v2

--- a/solution.py
+++ b/solution.py
@@ -53,6 +53,10 @@
     high = table.astype(BF16)
     low = (table - high.astype(np.float32)).astype(BF16)
     return np.concatenate([high, low], axis=0)
+
+
+def hops(step, around):
+    return min(step, around - step)
 
 
 def mm(a, b):
@@ -155,6 +159,14 @@
     def at_y(step):
         return (gx, lax.rem(gy + (step + ny), ny))
 
+    barrier = pltpu.get_barrier_semaphore()
+    x_steps = sorted(range(1, nx), key=lambda s: -hops(s % 4, 4) - hops(s // 4, nx // 4))
+    y_steps = sorted(range(1, ny), key=lambda s: -hops(s, ny))
+    for step in x_steps:
+        pl.semaphore_signal(barrier, inc=1, device_id=at_x(step), device_id_type=MESH)
+    for step in y_steps:
+        pl.semaphore_signal(barrier, inc=1, device_id=at_y(step), device_id_type=MESH)
+
     pairs = (
         (flow_hbm, flow),
         (interp_hbm, interp),
@@ -173,11 +185,6 @@
     ]
     for copy in loading:
         copy.start()
-    barrier = pltpu.get_barrier_semaphore()
-    for step in range(1, ny):
-        pl.semaphore_signal(barrier, inc=1, device_id=at_y(step), device_id_type=MESH)
-    for step in range(1, nx):
-        pl.semaphore_signal(barrier, inc=1, device_id=at_x(step), device_id_type=MESH)
     for copy in loading[:3]:
         copy.wait()
 
@@ -219,7 +226,7 @@
     pl.semaphore_wait(barrier, nx + ny - 2)
 
     first = []
-    for step in range(1, ny):
+    for step in y_steps:
         target = at_y(step)
         copy = pltpu.make_async_remote_copy(
             src_ref=sbuf.at[target[1]],
@@ -255,7 +262,7 @@
     for x in range(nx):
         mid[x] = r1[:, x, :]
     second = []
-    for step in range(1, nx):
+    for step in x_steps:
         target = at_x(step)
         copy = pltpu.make_async_remote_copy(
             src_ref=mid.at[target[0]],

time: 46.2 us -> 45.8 us (level)
  no operation moved by 1% of the time
where the time goes in v3:
time: 45.8 us; the launch traced here: 45.6 us
  Pallas kernels  43.9 us (96%)
  local copies, waits for them, and re-layouts  1.67 us (4%)
    pallas_call x1, Pallas kernels, shards(): pl.pallas_call(functools.partial(kernel, nx, ny), out_shape=jax.ShapeDtyp...  43.9 us
    unnamed x1, local copies, waits for them, and re-layouts  1.67 us

profile of v3, /device:TPU:0, one launch (start us, length us, event | category | flops | bytes accessed | tf_op | source)
XLA Modules:
  0.0 45.6 jit_solution(2722611018226470342)
XLA Ops:
  0.0 43.9 %shard_map.109 = bf16[1024,128]{1,0:T(8,128)(2,1)} custom-call(f32[8,4,512]{2,1,0:T(4,128)} %flow_hbm.1, bf16[128,512]{1,0:T(8,128)(2,1)} %constant.2.clone.interp_hbm, s32[1,8,128]{2,1,0:T(8,128)} %bitcast.1, s32[8,1024]{1,0:T(8,128)} %links_hbm.1, s32[1,2,2,64]{3,2,1,0:T(2,128)} %halo_hbm.1, f32[4,128]{1,0:T(4,128)} %enc_first_hbm.1, ...), custom_call_target="tpu_custom_call" | custom-call | tf_op jit(solution)/shard_map/pallas_call | solution.py:473
  43.9 1.7 %copy.13 = bf16[1024,128]{1,0:T(8,128)(2,1)} copy(bf16[1024,128]{1,0:T(8,128)(2,1)} %shard_map.109) | data formatting | bytes 524288

commit v4 on v3

--- a/solution.py
+++ b/solution.py
@@ -160,13 +160,6 @@
         return (gx, lax.rem(gy + (step + ny), ny))
 
     barrier = pltpu.get_barrier_semaphore()
-    x_steps = sorted(range(1, nx), key=lambda s: -hops(s % 4, 4) - hops(s // 4, nx // 4))
-    y_steps = sorted(range(1, ny), key=lambda s: -hops(s, ny))
-    for step in x_steps:
-        pl.semaphore_signal(barrier, inc=1, device_id=at_x(step), device_id_type=MESH)
-    for step in y_steps:
-        pl.semaphore_signal(barrier, inc=1, device_id=at_y(step), device_id_type=MESH)
-
     pairs = (
         (flow_hbm, flow),
         (interp_hbm, interp),
@@ -183,7 +176,15 @@
     loading = [
         pltpu.make_async_copy(there, here, loads.at[i]) for i, (there, here) in enumerate(pairs)
     ]
-    for copy in loading:
+    for copy in loading[:3]:
+        copy.start()
+    x_steps = sorted(range(1, nx), key=lambda s: -hops(s % 4, 4) - hops(s // 4, nx // 4))
+    y_steps = sorted(range(1, ny), key=lambda s: -hops(s, ny))
+    for step in x_steps:
+        pl.semaphore_signal(barrier, inc=1, device_id=at_x(step), device_id_type=MESH)
+    for step in y_steps:
+        pl.semaphore_signal(barrier, inc=1, device_id=at_y(step), device_id_type=MESH)
+    for copy in loading[3:]:
         copy.start()
     for copy in loading[:3]:
         copy.wait()

time: 45.8 us -> 45.8 us (level)
  no operation moved by 1% of the time
where the time goes in v4:
time: 45.8 us; the launch traced here: 45.6 us
  Pallas kernels  43.9 us (96%)
  local copies, waits for them, and re-layouts  1.67 us (4%)
    pallas_call x1, Pallas kernels, shards(): pl.pallas_call(functools.partial(kernel, nx, ny), out_shape=jax.ShapeDtyp...  43.9 us
    unnamed x1, local copies, waits for them, and re-layouts  1.67 us

profile of v4, /device:TPU:0, one launch (start us, length us, event | category | flops | bytes accessed | tf_op | source)
XLA Modules:
  0.0 45.6 jit_solution(9247827325867227206)
XLA Ops:
  0.0 43.9 %shard_map.109 = bf16[1024,128]{1,0:T(8,128)(2,1)} custom-call(f32[8,4,512]{2,1,0:T(4,128)} %flow_hbm.1, bf16[128,512]{1,0:T(8,128)(2,1)} %constant.2.clone.interp_hbm, s32[1,8,128]{2,1,0:T(8,128)} %bitcast.1, s32[8,1024]{1,0:T(8,128)} %links_hbm.1, s32[1,2,2,64]{3,2,1,0:T(2,128)} %halo_hbm.1, f32[4,128]{1,0:T(4,128)} %enc_first_hbm.1, ...), custom_call_target="tpu_custom_call" | custom-call | tf_op jit(solution)/shard_map/pallas_call | solution.py:474
  43.9 1.7 %copy.13 = bf16[1024,128]{1,0:T(8,128)(2,1)} copy(bf16[1024,128]{1,0:T(8,128)(2,1)} %shard_map.109) | data formatting | bytes 524288
